TPU v7x, 256 devices: a whole 4x4x8 slice. The times are simulated.
256 devices in a mesh: kv: 64 (over z, y, core), tp: 4 (over x).
Axes of the slice: x: 4, y: 4, z: 8, core: 2. Of those that a mesh axis runs over, the one named last changes fastest.
Arguments:
- queries: bfloat16 [384, 8192], P('kv', 'tp'), may hold values from -200 to 200
- shared_prefix_keys: bfloat16 [262144, 1024], P('kv', 'tp'), may hold values from -18 to 18
- shared_prefix_values: bfloat16 [262144, 1024], P('kv', 'tp'), may hold values from -6 to 6
- kept: int32 [262144], P('kv'), may hold values 0 or 1
- row_suffix_keys: bfloat16 [384, 512, 1024], P('kv', None, 'tp'), may hold values from -30 to 30
- row_suffix_values: bfloat16 [384, 512, 1024], P('kv', None, 'tp'), may hold values from -6 to 6
- suffix_lengths: int32 [384], P('kv'), may hold values from 2 to 512, as said below
- out_weight: bfloat16 [8192, 8192], P('tp', 'kv'), may hold values from -0.0625 to 0.0625
Outputs:
- projected: bfloat16 [384, 8192], P('tp', 'kv')
Inputs may be any that keep to these rules, and one draw needn't show every extreme that they name: `suffix_lengths`: live suffix positions of a row are its first ones; some row has exactly 512.
All inputs are finite; a program needn't handle non-finite values. No bound on the sum of `kept` on one device may be relied on, other than what follows from the above.
Results may differ from a plain program's by a relative error of at most 0.0065.
Values may be sent and summed in bfloat16 or wider, within the bound.
A program may use at most 128 MiB of HBM per device.

v0:
```python
import math

import jax
import jax.numpy as jnp
from jax import lax
from jax.sharding import PartitionSpec as P

HEAD_SIZE = 128


def prefix_partial(q_rows, keys, values, kept, scale):
    count = q_rows.shape[0]
    heads_kv = keys.shape[1] // HEAD_SIZE
    query_group = q_rows.shape[1] // (heads_kv * HEAD_SIZE)
    block = math.gcd(count, 32)
    keys3 = keys.reshape(-1, heads_kv, HEAD_SIZE)
    values3 = values.reshape(-1, heads_kv, HEAD_SIZE)
    live = (kept > 0)[None, None, None, :]

    def one_block(q_block):
        query_grouped = q_block.reshape(block, heads_kv, query_group, HEAD_SIZE)
        scores = (
            jnp.einsum("rhgd,khd->rhgk", query_grouped, keys3, preferred_element_type=jnp.float32)
            * scale
        )
        scores = jnp.where(live, scores, -jnp.inf)
        top = jnp.max(scores, axis=-1)
        weights = jnp.where(live, jnp.exp(scores - top[..., None]), 0.0).astype(jnp.bfloat16)
        numer = jnp.einsum("rhgk,khd->rhgd", weights, values3, preferred_element_type=jnp.float32)
        denom = jnp.sum(weights.astype(jnp.float32), axis=-1)
        return (numer.reshape(block, -1), top.reshape(block, -1), denom.reshape(block, -1))

    numer, top, denom = lax.map(one_block, q_rows.reshape(count // block, block, -1))
    return (numer.reshape(count, -1), top.reshape(count, -1), denom.reshape(count, -1))


def suffix_partial(q_rows, keys, values, lengths, scale):
    count = q_rows.shape[0]
    span = keys.shape[1]
    heads_kv = keys.shape[2] // HEAD_SIZE
    query_group = q_rows.shape[1] // (heads_kv * HEAD_SIZE)
    query_grouped = q_rows.reshape(count, heads_kv, query_group, HEAD_SIZE)
    keys4 = keys.reshape(count, span, heads_kv, HEAD_SIZE)
    values4 = values.reshape(count, span, heads_kv, HEAD_SIZE)
    scores = (
        jnp.einsum("rhgd,rkhd->rhgk", query_grouped, keys4, preferred_element_type=jnp.float32)
        * scale
    )
    live = (jnp.arange(span, dtype=jnp.int32)[None, :] < lengths[:, None])[:, None, None, :]
    scores = jnp.where(live, scores, -jnp.inf)
    top = jnp.max(scores, axis=-1)
    weights = jnp.where(live, jnp.exp(scores - top[..., None]), 0.0).astype(jnp.bfloat16)
    numer = jnp.einsum("rhgk,rkhd->rhgd", weights, values4, preferred_element_type=jnp.float32)
    denom = jnp.sum(weights.astype(jnp.float32), axis=-1)
    return (numer.reshape(count, -1, HEAD_SIZE), top.reshape(count, -1), denom.reshape(count, -1))


def per_device(
    queries,
    shared_prefix_keys,
    shared_prefix_values,
    kept,
    row_suffix_keys,
    row_suffix_values,
    suffix_lengths,
    out_weight,
):
    scale = HEAD_SIZE ** (-0.5)
    own_rows = queries.shape[0]
    heads = queries.shape[1] // HEAD_SIZE
    all_queries = lax.all_gather(queries, "kv", axis=0, tiled=True)
    numer_p, top_p, denom_p = prefix_partial(
        all_queries, shared_prefix_keys, shared_prefix_values, kept, scale
    )
    numer_s, top_s, denom_s = suffix_partial(
        queries, row_suffix_keys, row_suffix_values, suffix_lengths, scale
    )
    numer_r, top_r, denom_r = (
        lax.all_to_all(numer_p, "kv", split_axis=0, concat_axis=0, tiled=True),
        lax.all_to_all(top_p, "kv", split_axis=0, concat_axis=0, tiled=True),
        lax.all_to_all(denom_p, "kv", split_axis=0, concat_axis=0, tiled=True),
    )
    peers = numer_r.shape[0] // own_rows
    numer_r = numer_r.reshape(peers, own_rows, heads, HEAD_SIZE)
    top_r = top_r.reshape(peers, own_rows, heads)
    denom_r = denom_r.reshape(peers, own_rows, heads)
    best = jnp.maximum(jnp.max(top_r, axis=0), top_s)
    scale_r = jnp.exp(top_r - best[None])
    scale_s = jnp.exp(top_s - best)
    numer = jnp.sum(numer_r * scale_r[..., None], axis=0) + numer_s * scale_s[..., None]
    denom = jnp.sum(denom_r * scale_r, axis=0) + denom_s * scale_s
    merged = (numer / denom[..., None]).reshape(own_rows, heads * HEAD_SIZE).astype(jnp.bfloat16)
    attention = lax.all_gather(merged, "kv", axis=0, tiled=True)
    projected = lax.psum_scatter(
        jnp.dot(attention, out_weight, preferred_element_type=jnp.float32),
        "tp",
        scatter_dimension=0,
        tiled=True,
    )
    return projected.astype(jnp.bfloat16)


def solution(mesh):
    return jax.shard_map(
        per_device,
        mesh=mesh,
        in_specs=(
            P("kv", "tp"),
            P("kv", "tp"),
            P("kv", "tp"),
            P("kv"),
            P("kv", None, "tp"),
            P("kv", None, "tp"),
            P("kv"),
            P("tp", "kv"),
        ),
        out_specs=P("tp", "kv"),
        check_vma=False,
    )
```

profile of v0, /device:TPU:1, one launch (start us, length us, event | category | flops | bytes accessed | tf_op | source)
XLA Modules:
  0.0 550.4 jit_solution(9493258134851178774)
XLA Ops:
  24.4 67.3 %all-gather.5.cloned.1.call-done = bf16[64,6,2048]{2,1,0:T(8,128)(2,1)} async-done(((bf16[1,6,2048]{2,1,0:T(8,128)(2,1)}), bf16[64,6,2048]{2,1,0:T(8,128)(2,1)}) %all-gather.5.cloned.1.call-update) | async-done | bytes 1572880 | tf_op jit(solution)/shard_map/all_gather | solution.py:71
  95.4 203.8 %while.14 = (s32[]{:T(128)}, f32[12,32,2048]{2,1,0:T(8,128)}, f32[12,32,16]{1,2,0:T(8,128)S(1)}, f32[12,32,16]{1,2,0:T(8,128)S(1)}, pred[1,1,1,4096]{3,2,1,0:T(4...) while((s32[]{:T(128)}, f32[12,32,2048]{2,1,0:T(8,128)}, ...), condition=%wide.region_3.4_spmd, body=%wide.region_0.3_spmd.sunk | while | flops 1105198080 | bytes 65474708 | solution.py:33
  96.4 6.1 %bitcast_reduce_fusion.2 = (f32[32,2,8]{2,0,1:T(8,128)S(1)}, f32[2,32,8,4096]{3,2,1,0:T(8,128)}) fusion(pred[4096]{0:T(1024)(128)(4,1)S(1)} %reduce.4, bf16[4096,2,128]{2,0,1:T(8,128)(2,1)} %get-tuple-element.187, bf16[32,2,8,128]{3,2,1,0:T(8,128)(2,1)S(1)} %bitcast.122), kind=kOutput, calls=%fused_computation.1.clone.1 | convolution fusion | flops 543161856 | bytes 10622976 | tf_op jit(solution)/shard_map/while/body/eval_jaxpr/rhgd,khd->rhgk/dot_general | solution.py:23
  102.6 5.4 convert_reduce_fusion.3
  113.4 6.1 %bitcast_reduce_fusion.2 = (f32[32,2,8]{2,0,1:T(8,128)S(1)}, f32[2,32,8,4096]{3,2,1,0:T(8,128)}) fusion(pred[4096]{0:T(1024)(128)(4,1)S(1)} %reduce.4, bf16[4096,2,128]{2,0,1:T(8,128)(2,1)} %get-tuple-element.187, bf16[32,2,8,128]{3,2,1,0:T(8,128)(2,1)S(1)} %bitcast.122), kind=kOutput, calls=%fused_computation.1.clone.1 | convolution fusion | flops 543161856 | bytes 10622976 | tf_op jit(solution)/shard_map/while/body/eval_jaxpr/rhgd,khd->rhgk/dot_general | solution.py:23
  119.5 5.4 convert_reduce_fusion.3
  130.4 6.1 %bitcast_reduce_fusion.2 = (f32[32,2,8]{2,0,1:T(8,128)S(1)}, f32[2,32,8,4096]{3,2,1,0:T(8,128)}) fusion(pred[4096]{0:T(1024)(128)(4,1)S(1)} %reduce.4, bf16[4096,2,128]{2,0,1:T(8,128)(2,1)} %get-tuple-element.187, bf16[32,2,8,128]{3,2,1,0:T(8,128)(2,1)S(1)} %bitcast.122), kind=kOutput, calls=%fused_computation.1.clone.1 | convolution fusion | flops 543161856 | bytes 10622976 | tf_op jit(solution)/shard_map/while/body/eval_jaxpr/rhgd,khd->rhgk/dot_general | solution.py:23
  136.5 5.4 convert_reduce_fusion.3
  147.4 6.1 %bitcast_reduce_fusion.2 = (f32[32,2,8]{2,0,1:T(8,128)S(1)}, f32[2,32,8,4096]{3,2,1,0:T(8,128)}) fusion(pred[4096]{0:T(1024)(128)(4,1)S(1)} %reduce.4, bf16[4096,2,128]{2,0,1:T(8,128)(2,1)} %get-tuple-element.187, bf16[32,2,8,128]{3,2,1,0:T(8,128)(2,1)S(1)} %bitcast.122), kind=kOutput, calls=%fused_computation.1.clone.1 | convolution fusion | flops 543161856 | bytes 10622976 | tf_op jit(solution)/shard_map/while/body/eval_jaxpr/rhgd,khd->rhgk/dot_general | solution.py:23
  153.5 5.4 convert_reduce_fusion.3
  164.4 6.1 %bitcast_reduce_fusion.2 = (f32[32,2,8]{2,0,1:T(8,128)S(1)}, f32[2,32,8,4096]{3,2,1,0:T(8,128)}) fusion(pred[4096]{0:T(1024)(128)(4,1)S(1)} %reduce.4, bf16[4096,2,128]{2,0,1:T(8,128)(2,1)} %get-tuple-element.187, bf16[32,2,8,128]{3,2,1,0:T(8,128)(2,1)S(1)} %bitcast.122), kind=kOutput, calls=%fused_computation.1.clone.1 | convolution fusion | flops 543161856 | bytes 10622976 | tf_op jit(solution)/shard_map/while/body/eval_jaxpr/rhgd,khd->rhgk/dot_general | solution.py:23
  170.5 5.4 convert_reduce_fusion.3
  181.3 6.1 %bitcast_reduce_fusion.2 = (f32[32,2,8]{2,0,1:T(8,128)S(1)}, f32[2,32,8,4096]{3,2,1,0:T(8,128)}) fusion(pred[4096]{0:T(1024)(128)(4,1)S(1)} %reduce.4, bf16[4096,2,128]{2,0,1:T(8,128)(2,1)} %get-tuple-element.187, bf16[32,2,8,128]{3,2,1,0:T(8,128)(2,1)S(1)} %bitcast.122), kind=kOutput, calls=%fused_computation.1.clone.1 | convolution fusion | flops 543161856 | bytes 10622976 | tf_op jit(solution)/shard_map/while/body/eval_jaxpr/rhgd,khd->rhgk/dot_general | solution.py:23
  187.5 5.4 convert_reduce_fusion.3
  198.3 6.1 %bitcast_reduce_fusion.2 = (f32[32,2,8]{2,0,1:T(8,128)S(1)}, f32[2,32,8,4096]{3,2,1,0:T(8,128)}) fusion(pred[4096]{0:T(1024)(128)(4,1)S(1)} %reduce.4, bf16[4096,2,128]{2,0,1:T(8,128)(2,1)} %get-tuple-element.187, bf16[32,2,8,128]{3,2,1,0:T(8,128)(2,1)S(1)} %bitcast.122), kind=kOutput, calls=%fused_computation.1.clone.1 | convolution fusion | flops 543161856 | bytes 10622976 | tf_op jit(solution)/shard_map/while/body/eval_jaxpr/rhgd,khd->rhgk/dot_general | solution.py:23
  204.5 5.4 convert_reduce_fusion.3
  215.3 6.1 %bitcast_reduce_fusion.2 = (f32[32,2,8]{2,0,1:T(8,128)S(1)}, f32[2,32,8,4096]{3,2,1,0:T(8,128)}) fusion(pred[4096]{0:T(1024)(128)(4,1)S(1)} %reduce.4, bf16[4096,2,128]{2,0,1:T(8,128)(2,1)} %get-tuple-element.187, bf16[32,2,8,128]{3,2,1,0:T(8,128)(2,1)S(1)} %bitcast.122), kind=kOutput, calls=%fused_computation.1.clone.1 | convolution fusion | flops 543161856 | bytes 10622976 | tf_op jit(solution)/shard_map/while/body/eval_jaxpr/rhgd,khd->rhgk/dot_general | solution.py:23
  221.5 5.4 convert_reduce_fusion.3
  232.3 6.1 %bitcast_reduce_fusion.2 = (f32[32,2,8]{2,0,1:T(8,128)S(1)}, f32[2,32,8,4096]{3,2,1,0:T(8,128)}) fusion(pred[4096]{0:T(1024)(128)(4,1)S(1)} %reduce.4, bf16[4096,2,128]{2,0,1:T(8,128)(2,1)} %get-tuple-element.187, bf16[32,2,8,128]{3,2,1,0:T(8,128)(2,1)S(1)} %bitcast.122), kind=kOutput, calls=%fused_computation.1.clone.1 | convolution fusion | flops 543161856 | bytes 10622976 | tf_op jit(solution)/shard_map/while/body/eval_jaxpr/rhgd,khd->rhgk/dot_general | solution.py:23
  238.5 5.4 convert_reduce_fusion.3
  249.3 6.1 %bitcast_reduce_fusion.2 = (f32[32,2,8]{2,0,1:T(8,128)S(1)}, f32[2,32,8,4096]{3,2,1,0:T(8,128)}) fusion(pred[4096]{0:T(1024)(128)(4,1)S(1)} %reduce.4, bf16[4096,2,128]{2,0,1:T(8,128)(2,1)} %get-tuple-element.187, bf16[32,2,8,128]{3,2,1,0:T(8,128)(2,1)S(1)} %bitcast.122), kind=kOutput, calls=%fused_computation.1.clone.1 | convolution fusion | flops 543161856 | bytes 10622976 | tf_op jit(solution)/shard_map/while/body/eval_jaxpr/rhgd,khd->rhgk/dot_general | solution.py:23
  266.3 6.1 %bitcast_reduce_fusion.2 = (f32[32,2,8]{2,0,1:T(8,128)S(1)}, f32[2,32,8,4096]{3,2,1,0:T(8,128)}) fusion(pred[4096]{0:T(1024)(128)(4,1)S(1)} %reduce.4, bf16[4096,2,128]{2,0,1:T(8,128)(2,1)} %get-tuple-element.187, bf16[32,2,8,128]{3,2,1,0:T(8,128)(2,1)S(1)} %bitcast.122), kind=kOutput, calls=%fused_computation.1.clone.1 | convolution fusion | flops 543161856 | bytes 10622976 | tf_op jit(solution)/shard_map/while/body/eval_jaxpr/rhgd,khd->rhgk/dot_general | solution.py:23
  272.4 5.4 convert_reduce_fusion.3
  283.3 6.1 %bitcast_reduce_fusion.2 = (f32[32,2,8]{2,0,1:T(8,128)S(1)}, f32[2,32,8,4096]{3,2,1,0:T(8,128)}) fusion(pred[4096]{0:T(1024)(128)(4,1)S(1)} %reduce.4, bf16[4096,2,128]{2,0,1:T(8,128)(2,1)} %get-tuple-element.187, bf16[32,2,8,128]{3,2,1,0:T(8,128)(2,1)S(1)} %bitcast.122), kind=kOutput, calls=%fused_computation.1.clone.1 | convolution fusion | flops 543161856 | bytes 10622976 | tf_op jit(solution)/shard_map/while/body/eval_jaxpr/rhgd,khd->rhgk/dot_general | solution.py:23
  289.4 5.4 convert_reduce_fusion.3
  300.1 6.6 %all-to-all-start.2 = ((f32[64,6,16]{2,1,0:T(8,128)}), f32[64,6,16]{2,1,0:T(8,128)S(1)}, u32[]{:S(2)}, u32[]{:S(2)}) async-start(f32[64,6,16]{2,1,0:T(8,128)} %all_to_all.22), calls=%async_computation.2 | async-start | bytes 524288 | tf_op jit(solution)/shard_map/all_to_all | solution.py:81
  307.5 12.3 %all-to-all-done.2 = f32[64,6,16]{2,1,0:T(8,128)S(1)} async-done(((f32[64,6,16]{2,1,0:T(8,128)}), f32[64,6,16]{2,1,0:T(8,128)S(1)}, u32[]{:S(2)}, u32[]{:S(2)}) %all-to-all-start.2) | async-done | bytes 24608 | tf_op jit(solution)/shard_map/all_to_all | solution.py:81
  329.2 8.6 %all-to-all-done.1 = f32[64,6,16]{2,1,0:T(8,128)S(1)} async-done(((f32[64,6,16]{2,1,0:T(8,128)}), f32[64,6,16]{2,1,0:T(8,128)S(1)}, u32[]{:S(2)}, u32[]{:S(2)}) %all-to-all-start.1) | async-done | bytes 24608 | tf_op jit(solution)/shard_map/all_to_all | solution.py:80
  353.2 84.5 %all-to-all-done = f32[64,6,2048]{2,1,0:T(8,128)} async-done(((f32[64,6,2048]{2,1,0:T(8,128)}), f32[64,6,2048]{2,1,0:T(8,128)}, u32[]{:S(2)}, u32[]{:S(2)}) %all-to-all-start) | async-done | bytes 3145760 | tf_op jit(solution)/shard_map/all_to_all | solution.py:79
  437.7 5.5 fusion.12
  443.9 75.4 %all-gather.7.cloned.1.call-done = bf16[64,6,2048]{2,1,0:T(8,128)(2,1)} async-done(((bf16[1,6,2048]{2,1,0:T(8,128)(2,1)}), bf16[64,6,2048]{2,1,0:T(8,128)(2,1)}) %all-gather.7.cloned.1.call-update) | async-done | bytes 1572880 | tf_op jit(solution)/shard_map/all_gather | solution.py:93
  524.3 18.2 %reduce-scatter.2.cloned.1.call-done = f32[96,128]{1,0:T(8,128)} async-done(((f32[384,128]{1,0:T(8,128)}), f32[96,128]{1,0:T(8,128)}) %reduce-scatter.2.cloned.1.call-update) | async-done | bytes 49168 | tf_op jit(solution)/shard_map/reduce_scatter | solution.py:94
  (192 shorter events, 126.0 us)
Async XLA Ops:
  6.5 336.8 %copy-start = (bf16[6,512,256]{2,1,0:T(8,128)(2,1)S(1)}, bf16[6,512,256]{2,1,0:T(8,128)(2,1)}, u32[]{:S(2)}) copy-start(bf16[6,512,256]{2,1,0:T(8,128)(2,1)} %param.14) | copy-start | bytes 4718596
  6.5 85.1 %all-gather.5.cloned.1.call-start = ((), (), s32[]{:S(2)}) async-start(), calls=%async_computation.5 | async-start | bytes 2129920 | tf_op jit(solution)/shard_map/all_gather | solution.py:71
  102.6 5.8 %copy-start.1 = (f32[2,32,8,4096]{3,2,1,0:T(8,128)S(1)}, f32[2,32,8,4096]{3,2,1,0:T(8,128)}, u32[]{:S(2)}) copy-start(f32[2,32,8,4096]{3,2,1,0:T(8,128)} %get-tuple-element.157) | copy-start | bytes 25165828 | tf_op jit(solution)/shard_map/while
  119.5 5.8 %copy-start.1 = (f32[2,32,8,4096]{3,2,1,0:T(8,128)S(1)}, f32[2,32,8,4096]{3,2,1,0:T(8,128)}, u32[]{:S(2)}) copy-start(f32[2,32,8,4096]{3,2,1,0:T(8,128)} %get-tuple-element.157) | copy-start | bytes 25165828 | tf_op jit(solution)/shard_map/while
  136.5 5.8 %copy-start.1 = (f32[2,32,8,4096]{3,2,1,0:T(8,128)S(1)}, f32[2,32,8,4096]{3,2,1,0:T(8,128)}, u32[]{:S(2)}) copy-start(f32[2,32,8,4096]{3,2,1,0:T(8,128)} %get-tuple-element.157) | copy-start | bytes 25165828 | tf_op jit(solution)/shard_map/while
  153.5 5.8 %copy-start.1 = (f32[2,32,8,4096]{3,2,1,0:T(8,128)S(1)}, f32[2,32,8,4096]{3,2,1,0:T(8,128)}, u32[]{:S(2)}) copy-start(f32[2,32,8,4096]{3,2,1,0:T(8,128)} %get-tuple-element.157) | copy-start | bytes 25165828 | tf_op jit(solution)/shard_map/while
  170.5 5.8 %copy-start.1 = (f32[2,32,8,4096]{3,2,1,0:T(8,128)S(1)}, f32[2,32,8,4096]{3,2,1,0:T(8,128)}, u32[]{:S(2)}) copy-start(f32[2,32,8,4096]{3,2,1,0:T(8,128)} %get-tuple-element.157) | copy-start | bytes 25165828 | tf_op jit(solution)/shard_map/while
  187.5 5.8 %copy-start.1 = (f32[2,32,8,4096]{3,2,1,0:T(8,128)S(1)}, f32[2,32,8,4096]{3,2,1,0:T(8,128)}, u32[]{:S(2)}) copy-start(f32[2,32,8,4096]{3,2,1,0:T(8,128)} %get-tuple-element.157) | copy-start | bytes 25165828 | tf_op jit(solution)/shard_map/while
  204.5 5.8 %copy-start.1 = (f32[2,32,8,4096]{3,2,1,0:T(8,128)S(1)}, f32[2,32,8,4096]{3,2,1,0:T(8,128)}, u32[]{:S(2)}) copy-start(f32[2,32,8,4096]{3,2,1,0:T(8,128)} %get-tuple-element.157) | copy-start | bytes 25165828 | tf_op jit(solution)/shard_map/while
  221.5 5.8 %copy-start.1 = (f32[2,32,8,4096]{3,2,1,0:T(8,128)S(1)}, f32[2,32,8,4096]{3,2,1,0:T(8,128)}, u32[]{:S(2)}) copy-start(f32[2,32,8,4096]{3,2,1,0:T(8,128)} %get-tuple-element.157) | copy-start | bytes 25165828 | tf_op jit(solution)/shard_map/while
  238.5 5.8 %copy-start.1 = (f32[2,32,8,4096]{3,2,1,0:T(8,128)S(1)}, f32[2,32,8,4096]{3,2,1,0:T(8,128)}, u32[]{:S(2)}) copy-start(f32[2,32,8,4096]{3,2,1,0:T(8,128)} %get-tuple-element.157) | copy-start | bytes 25165828 | tf_op jit(solution)/shard_map/while
  255.5 5.8 %copy-start.1 = (f32[2,32,8,4096]{3,2,1,0:T(8,128)S(1)}, f32[2,32,8,4096]{3,2,1,0:T(8,128)}, u32[]{:S(2)}) copy-start(f32[2,32,8,4096]{3,2,1,0:T(8,128)} %get-tuple-element.157) | copy-start | bytes 25165828 | tf_op jit(solution)/shard_map/while
  272.4 5.8 %copy-start.1 = (f32[2,32,8,4096]{3,2,1,0:T(8,128)S(1)}, f32[2,32,8,4096]{3,2,1,0:T(8,128)}, u32[]{:S(2)}) copy-start(f32[2,32,8,4096]{3,2,1,0:T(8,128)} %get-tuple-element.157) | copy-start | bytes 25165828 | tf_op jit(solution)/shard_map/while
  289.4 5.8 %copy-start.1 = (f32[2,32,8,4096]{3,2,1,0:T(8,128)S(1)}, f32[2,32,8,4096]{3,2,1,0:T(8,128)}, u32[]{:S(2)}) copy-start(f32[2,32,8,4096]{3,2,1,0:T(8,128)} %get-tuple-element.157) | copy-start | bytes 25165828 | tf_op jit(solution)/shard_map/while
  300.1 19.8 %all-to-all-start.2 = ((f32[64,6,16]{2,1,0:T(8,128)}), f32[64,6,16]{2,1,0:T(8,128)S(1)}, u32[]{:S(2)}, u32[]{:S(2)}) async-start(f32[64,6,16]{2,1,0:T(8,128)} %all_to_all.22), calls=%async_computation.2 | async-start | bytes 524288 | tf_op jit(solution)/shard_map/all_to_all | solution.py:81
  319.9 17.9 %all-to-all-start.1 = ((f32[64,6,16]{2,1,0:T(8,128)}), f32[64,6,16]{2,1,0:T(8,128)S(1)}, u32[]{:S(2)}, u32[]{:S(2)}) async-start(f32[64,6,16]{2,1,0:T(8,128)} %all_to_all.20), calls=%async_computation.1 | async-start | bytes 524288 | tf_op jit(solution)/shard_map/all_to_all | solution.py:80
  329.2 14.1 %copy-start.3 = (s32[6]{0:T(128)S(1)}, s32[6]{0:T(128)}, u32[]{:S(2)}) copy-start(s32[6]{0:T(128)} %param.16) | copy-start | bytes 76
  329.2 14.2 %copy-start.2 = (bf16[6,2048]{1,0:T(8,128)(2,1)S(1)}, bf16[6,2048]{1,0:T(8,128)(2,1)}, u32[]{:S(2)}) copy-start(bf16[6,2048]{1,0:T(8,128)(2,1)} %param.10) | copy-start | bytes 73732
  337.7 100.0 %all-to-all-start = ((f32[64,6,2048]{2,1,0:T(8,128)}), f32[64,6,2048]{2,1,0:T(8,128)}, u32[]{:S(2)}, u32[]{:S(2)}) async-start(f32[64,6,2048]{2,1,0:T(8,128)} %all_to_all.18), calls=%async_computation | async-start | bytes 8388608 | tf_op jit(solution)/shard_map/all_to_all | solution.py:79
  343.0 176.3 %all-gather.7.cloned.1.call-start = ((), (), s32[]{:S(2)}) async-start(), calls=%async_computation.6 | async-start | bytes 2129920 | tf_op jit(solution)/shard_map/all_gather | solution.py:93
  443.9 98.6 %reduce-scatter.2.cloned.1.call-start = ((), (), s32[]{:S(2)}) async-start(), calls=%async_computation.4 | async-start | bytes 245760 | tf_op jit(solution)/shard_map/reduce_scatter | solution.py:94
Sparse Core Ops, SparseCore 0:
  10.1 81.5 all-gather.4
  444.0 75.3 all-gather.6
  524.4 18.0 reduce-scatter.1
where the time goes:
time: 554 us; the launch traced here: 550 us
  waiting for transfers between devices  267 us (48%)
  matrix products  115 us (21%)
  other arithmetic  73.8 us (13%)
  local copies, waits for them, and re-layouts  64.2 us (12%)
  starting transfers between devices  16.9 us (3%)
  between operations  13.2 us (2%)
    all_to_all x1, waiting for transfers between devices, per_device(): lax.all_to_all(numer_p, 'kv', split_axis=0, concat_axis=0, tiled=True)  84.5 us
    all_gather x1, waiting for transfers between devices, per_device(): attention = lax.all_gather(merged, 'kv', axis=0, tiled=True)  75.4 us
    dot_general x12, matrix products, one_block(): jnp.einsum('rhgd,khd->rhgk', query_grouped, keys3, preferred_element_type...  73.2 us
    all_gather x1, waiting for transfers between devices, per_device(): all_queries = lax.all_gather(queries, 'kv', axis=0, tiled=True)  67.3 us
    reduce_sum x12, other arithmetic, one_block(): denom = jnp.sum(weights.astype(jnp.float32), axis=-1)  64.5 us
    dot_general x12, matrix products, one_block(): jnp.einsum('rhgk,khd->rhgd', weights, values3, preferred_element_type=jnp...  36.8 us
    reduce_scatter x1, waiting for transfers between devices, per_device(): lax.psum_scatter(jnp.dot(attention, out_weight, preferred_element_type=jn...  18.2 us
    while x48, local copies, waits for them, and re-layouts  16.8 us
  transfers between devices with their start and end apart: 6, of which 6 were waited for; matrix products, arithmetic and copies ran while one was open for 5% of the time, Pallas kernels for 0%

commit v1 on v0

v1 whole, which is shorter than its diff:
```python
import jax
import jax.numpy as jnp
from jax import lax
from jax.experimental import pallas as pl
from jax.experimental.pallas import tpu as pltpu
from jax.sharding import PartitionSpec as P

MESH = pl.DeviceIdType.MESH
F32 = jnp.float32
BF16 = jnp.bfloat16
HD = 128
ROWS = 6
G = 8
QV = ROWS * G
KEYS = 4096
SPAN = 512
NZ, NY = 8, 4
HALF = NZ * QV
UNIT = 2 * HALF
TK = 512
VR = 144
C = float(HD**-0.5 * 1.4426950408889634)
DROPPED = -1e30


def merge(parts):
    top = parts[0][1]
    for _, lse in parts[1:]:
        top = jnp.maximum(top, lse)
    total, out = None, None
    for o, lse in parts:
        w = jnp.exp2(lse - top)
        total = w if total is None else total + w
        out = o * w if out is None else out + o * w
    return out * (1.0 / total), top + jnp.log2(total)


def split3(x):
    hi = x.astype(BF16).astype(F32)
    rest = x - hi
    mid = rest.astype(BF16).astype(F32)
    return hi, mid, rest - mid


def pack_t(o, lse):
    n = o.shape[1]
    hi, mid, lo = split3(lse)
    row = lax.broadcasted_iota(jnp.int32, (VR - HD, n), 0)
    stat = jnp.where(row == 0, hi, jnp.where(row == 1, mid, jnp.where(row == 2, lo, 0.0)))
    return jnp.concatenate([o, stat], axis=0).astype(BF16)


def unpack_t(x):
    x = x.astype(F32)
    return x[:HD], x[HD : HD + 1] + x[HD + 1 : HD + 2] + x[HD + 2 : HD + 3]


def unpack_r(x):
    x = x.astype(F32)
    return x[:, :HD], x[:, HD : HD + 1] + x[:, HD + 1 : HD + 2] + x[:, HD + 2 : HD + 3]


def kernel(
    q_ref, k_hbm, v_hbm, kept_ref, sk_hbm, sv_hbm, len_ref, w_hbm, out_ref,
    kbuf, vbuf, vt, bias, s0, s1, skbuf, svbuf, wbuf, qf, qg, rsout, sibin, ysend, yin, zout, zin,
    attg, attf, osuf, lsuf, part, tpin,
    load_sem, qz_s, qz_r, qy_s, qy_r, qs_s, qs_r, sib_s, sib_r, ry_s, ry_r, rz_s, rz_r,
    az_s, az_r, ay_s, ay_r, as_s, as_r, tp_s, tp_r,
):
    k = lax.axis_index("kv")
    x = lax.axis_index("tp")
    z, y, c = k // (2 * NY), (k // 2) % NY, k % 2

    def dev(zz, yy, cc):
        return ((zz * NY + yy) * 2 + cc, x)

    sibling = dev(z, y, 1 - c)

    def remote(src, dst, s, r, to):
        return pltpu.make_async_remote_copy(
            src_ref=src, dst_ref=dst, send_sem=s, recv_sem=r, device_id=to, device_id_type=MESH
        )

    loads = [
        pltpu.make_async_copy(sk_hbm, skbuf, load_sem.at[0]),
        pltpu.make_async_copy(sv_hbm, svbuf, load_sem.at[1]),
    ]
    for h in range(2):
        cols = slice(h * HD, (h + 1) * HD)
        loads.append(pltpu.make_async_copy(v_hbm.at[:, cols], vbuf.at[h], load_sem.at[2 + 2 * h]))
        loads.append(pltpu.make_async_copy(k_hbm.at[:, cols], kbuf.at[h], load_sem.at[3 + 2 * h]))
    loads.append(pltpu.make_async_copy(w_hbm, wbuf, load_sem.at[6]))
    for copy in loads:
        copy.start()

    own = q_ref[...].astype(F32)
    for h in range(2):
        for g in range(G):
            at = (h * G + g) * HD
            qf[h, pl.ds(g, ROWS, stride=G), :] = own[:, at : at + HD]
        qg[h, y, c, z] = qf[h].astype(BF16)

    barrier = pltpu.get_barrier_semaphore()
    peers = [sibling]
    peers += [dev(z, (y + i) % NY, c) for i in range(1, NY)]
    peers += [dev((z + i) % NZ, y, c) for i in range(1, NZ)]
    peers += [(k, (x + i) % 4) for i in range(1, 4)]
    for p in peers:
        pl.semaphore_signal(barrier, inc=1, device_id=p, device_id_type=MESH)
    pl.semaphore_wait(barrier, len(peers))

    def qz(h, i):
        blk = qg.at[h, y, c, z]
        return remote(blk, blk, qz_s.at[h, i], qz_r.at[h, i], dev((z + i) % NZ, y, c))

    def qz_arrival(h, i):
        blk = qg.at[h, y, c, (z + NZ - i) % NZ]
        return remote(blk, blk, qz_s.at[h, i], qz_r.at[h, i], dev((z + i) % NZ, y, c))

    def unit_offset(s):
        j = (s + s // 4) % 4
        return j + (j // 2) * (5 - 2 * j)

    def qy(s):
        blk = qg.at[s // 4, y, c]
        return remote(blk, blk, qy_s.at[s], qy_r.at[s], dev(z, (y + NY - unit_offset(s)) % NY, c))

    def qy_arrival(s):
        blk = qg.at[s // 4, (y + unit_offset(s)) % NY, c]
        return remote(blk, blk, qy_s.at[s], qy_r.at[s], sibling)

    def qs(s):
        blk = qg.at[s // 4, (y + unit_offset(s)) % NY, c]
        return remote(blk, blk, qs_s.at[s], qs_r.at[s], sibling)

    def qs_arrival(s):
        blk = qg.at[s // 4, (y + unit_offset(s)) % NY, 1 - c]
        return remote(blk, blk, qs_s.at[s], qs_r.at[s], sibling)

    def forward(s):
        qy_arrival(s).wait_recv()
        qs(s).start()

    for h in range(2):
        for i in (1, 7, 2, 6, 3, 5, 4):
            qz(h, i).start()

    kept = jnp.where(kept_ref[...] > 0, 0.0, DROPPED).astype(F32)
    kept = jnp.concatenate([kept, jnp.zeros((HD - KEYS // HD, HD), F32)], axis=0).T
    for j in range(KEYS // HD):
        bias[j * HD : (j + 1) * HD, :] = jnp.broadcast_to(kept[:, j : j + 1], (HD, HD)).astype(BF16)

    for h in range(2):
        loads[2 + 2 * h].wait()

        def turn(j, _, h=h):
            at = pl.multiple_of(j * 512, 512)
            vt[h, :HD, pl.ds(at, 512)] = vbuf[h, pl.ds(at, 512), :].astype(F32).T.astype(BF16)
            return 0

        lax.fori_loop(0, KEYS // 512, turn, 0)
        vt[h, HD:, :] = jnp.ones((VR - HD, KEYS), BF16)

    def spread(h):
        for i in range(1, NZ):
            qz_arrival(h, i).wait_recv()
        qs(7 * h).start()
        for s in (1, 2, 3):
            qy(3 * h + s).start()

    spread(0)

    loads[0].wait()
    loads[1].wait()
    for r in range(ROWS):
        live = lax.broadcasted_iota(jnp.int32, (G, SPAN), 1) < len_ref[r]
        for h in range(2):
            cols = slice(h * HD, (h + 1) * HD)
            q8 = qf[h, r * G : (r + 1) * G, :].astype(BF16)
            t = lax.dot_general(q8, skbuf[r, :, cols], (((1,), (1,)), ((), ())), preferred_element_type=F32)
            t = jnp.where(live, t * C, DROPPED)
            top = jnp.max(t, axis=1, keepdims=True)
            p = jnp.exp2(t - top).astype(BF16)
            total = jnp.sum(p.astype(F32), axis=1, keepdims=True)
            o = jnp.dot(p, svbuf[r, :, cols], preferred_element_type=F32)
            osuf[h, r * G : (r + 1) * G, :] = o * (1.0 / total)
            lsuf[h, r * G : (r + 1) * G, :] = jnp.broadcast_to(top + jnp.log2(total), (G, HD))

    spread(1)
    loads[3].wait()
    loads[5].wait()
    forward(1)
    qs_arrival(0).wait_recv()

    first_lane = (lax.broadcasted_iota(jnp.int32, (UNIT, HD), 1) == 0).astype(F32).astype(BF16)

    def unit_queries(s):
        q = qg[s // 4, (y + unit_offset(s)) % NY].reshape(UNIT, HD)
        return jnp.concatenate([q, first_lane], axis=1)

    def scores(s, q, t, buf, m8):
        rows = slice(t * TK, (t + 1) * TK)
        kt = jnp.concatenate([kbuf[s // 4, rows, :], bias[rows, :]], axis=1)
        sc = lax.dot_general(kt, q, (((1,), (1,)), ((), ())), preferred_element_type=F32)
        buf[rows, :] = sc
        return jnp.maximum(m8, jnp.max(sc.reshape(TK // 8, 8, UNIT), axis=0))

    def lowest():
        return jnp.full((8, UNIT), -3e38, F32)

    def stage(s, buf, nxt, m8):
        last = isinstance(s, int) and s == 7
        top = jnp.max(m8, axis=0, keepdims=True) * C
        q = None if last else unit_queries(s + 1)
        o = jnp.zeros((VR, UNIT), F32)
        m_next = lowest()
        for t in range(KEYS // TK):
            if not last:
                m_next = scores(s + 1, q, t, nxt, m_next)
            rows = slice(t * TK, (t + 1) * TK)
            p = jnp.exp2(buf[rows, :] * C - top).astype(BF16)
            o = o + jnp.dot(vt[s // 4, :, rows], p, preferred_element_type=F32)
        total = o[HD : HD + 1]
        done = pack_t(o[:HD] * (1.0 / total), top + jnp.log2(total))
        rsout[s, 0] = done[:, :HALF]
        rsout[s, 1] = done[:, HALF:]
        sib_send(s).start()
        return m_next

    def sib_send(s):
        return remote(rsout.at[s, 1 - c], sibin.at[s], sib_s.at[s], sib_r.at[s], sibling)

    def y_send(s):
        return remote(ysend.at[s], yin.at[s], ry_s.at[s], ry_r.at[s], dev(z, (y + unit_offset(s)) % NY, c))

    def sib_merge(s):
        sib_send(s).wait_recv()
        ysend[s] = pack_t(*merge([unpack_t(rsout[s, c]), unpack_t(sibin[s])]))

    def z_send(h, i):
        to = (z + i) % NZ
        return remote(zout.at[h, to], zin.at[h, i], rz_s.at[h, i], rz_r.at[h, i], dev(to, y, c))

    def y_merge(h):
        parts = [unpack_t(ysend[7 * h])]
        for s in (1, 2, 3):
            y_send(3 * h + s).wait_recv()
            parts.append(unpack_t(yin[3 * h + s]))
        o, lse = merge(parts)
        hi, mid, lo = split3(jnp.broadcast_to(lse, (HD, HALF)).T)
        lane = lax.broadcasted_iota(jnp.int32, (HALF, HD), 1)
        stat = jnp.where(lane == 0, hi, jnp.where(lane == 1, mid, jnp.where(lane == 2, lo, 0.0)))
        zout[h] = jnp.concatenate([o.T, stat], axis=1).astype(BF16).reshape(NZ, QV, 2 * HD)
        for i in (4, 3, 5, 2, 6, 1, 7):
            z_send(h, i).start()

    def az(h, i):
        blk = attg.at[h, z, y, c]
        return remote(blk, blk, az_s.at[h, i], az_r.at[h, i], dev((z + i) % NZ, y, c))

    def az_arrival(h, i):
        blk = attg.at[h, (z + NZ - i) % NZ, y, c]
        return remote(blk, blk, az_s.at[h, i], az_r.at[h, i], dev((z + i) % NZ, y, c))

    def z_merge(h):
        parts = [(osuf[h], lsuf[h][:, :1]), unpack_r(zout[h, z])]
        for i in range(1, NZ):
            z_send(h, i).wait_recv()
            parts.append(unpack_r(zin[h, i]))
        attg[h, z, y, c] = merge(parts)[0].astype(BF16)
        for i in (4, 3, 5, 2, 6, 1, 7):
            az(h, i).start()

    def ay(h, i):
        blk = attg.at[h, :, y, c]
        return remote(blk, blk, ay_s.at[h, i], ay_r.at[h, i], dev(z, (y + NY - i) % NY, c))

    def ay_arrival(h, i):
        blk = attg.at[h, :, (y + i) % NY, c]
        return remote(blk, blk, ay_s.at[h, i], ay_r.at[h, i], sibling)

    def a_sib(h, i):
        blk = attg.at[h, :, (y + i) % NY, c]
        return remote(blk, blk, as_s.at[h, i], as_r.at[h, i], sibling)

    def a_sib_arrival(h, i):
        blk = attg.at[h, :, (y + i) % NY, 1 - c]
        return remote(blk, blk, as_s.at[h, i], as_r.at[h, i], sibling)

    def gather_y(h):
        for i in range(1, NZ):
            az_arrival(h, i).wait_recv()
        for i in (2, 1, 3):
            ay(h, i).start()
        a_sib(h, 0).start()

    def gather_core(h):
        for i in (1, 3, 2):
            ay_arrival(h, i).wait_recv()
            a_sib(h, i).start()

    def project(h):
        for i in range(NY):
            a_sib_arrival(h, i).wait_recv()
        attf[...] = attg[h].reshape(-1, HD).astype(F32)
        rows = NZ * NY * 2 * ROWS
        att = jnp.concatenate([attf[pl.ds(g, rows, stride=G), :].astype(BF16) for g in range(G)], axis=1)
        return jnp.dot(att, wbuf[h * G * HD : (h + 1) * G * HD, :], preferred_element_type=F32)

    q = unit_queries(0)
    m8 = lowest()
    for t in range(KEYS // TK):
        m8 = scores(0, q, t, s0, m8)

    def pair(it, m8):
        a = 2 * it
        b = a + 1
        pl.when(it <= 2)(lambda: forward(a + 2))
        qs_arrival(b).wait_recv()
        m8 = stage(a, s0, s1, m8)

        @pl.when(it >= 1)
        def _():
            sib_merge(a - 1)
            y_send(a - 1).start()

        @pl.when(it == 3)
        def _():
            z_merge(0)

        @pl.when(it <= 1)
        def _():
            forward(b + 2)

        @pl.when(it <= 2)
        def _():
            qs_arrival(a + 2).wait_recv()

        m8 = stage(b, s1, s0, m8)
        sib_merge(a)

        @pl.when(it >= 1)
        def _():
            y_send(a).start()

        @pl.when(it == 2)
        def _():
            y_merge(0)

        return m8

    pair(3, lax.fori_loop(0, 3, pair, m8))

    gather_y(0)
    sib_merge(7)
    y_merge(1)
    gather_core(0)
    loads[6].wait()
    part[...] = project(0)
    z_merge(1)
    gather_y(1)
    gather_core(1)
    part[...] += project(1)

    per = part.shape[0] // 4

    def mine(xx):
        return part.at[pl.ds(pl.multiple_of(xx * per, 8), per), :]

    def tp_send(i):
        to = (x + i) % 4
        return remote(mine(to), tpin.at[i], tp_s.at[i], tp_r.at[i], (k, to))

    for i in range(1, 4):
        tp_send(i).start()
    total = part[pl.ds(pl.multiple_of(x * per, 8), per), :]
    for i in range(1, 4):
        tp_send(i).wait_recv()
        total = total + tpin[i]
    out_ref[...] = total.astype(BF16)

    for h in range(2):
        for i in range(1, NZ):
            qz(h, i).wait_send()
            z_send(h, i).wait_send()
            az(h, i).wait_send()
        for i in range(1, NY):
            ay(h, i).wait_send()
        for i in range(NY):
            a_sib(h, i).wait_send()
    for s in range(8):
        qs(s).wait_send()
        sib_send(s).wait_send()
        if 1 <= s <= 6:
            qy(s).wait_send()
            y_send(s).wait_send()
    for i in range(1, 4):
        tp_send(i).wait_send()


def per_device(queries, keys, values, kept, suffix_keys, suffix_values, lengths, out_weight):
    any_space = pl.BlockSpec(memory_space=pl.ANY)
    vmem = pl.BlockSpec(memory_space=pltpu.VMEM)
    sem = pltpu.SemaphoreType.DMA
    return pl.pallas_call(
        kernel,
        out_shape=jax.ShapeDtypeStruct((96, 128), BF16),
        in_specs=[
            vmem, any_space, any_space, vmem, any_space, any_space,
            pl.BlockSpec(memory_space=pltpu.SMEM), any_space,
        ],
        out_specs=vmem,
        scratch_shapes=[
            pltpu.VMEM((2, KEYS, HD), BF16),
            pltpu.VMEM((2, KEYS, HD), BF16),
            pltpu.VMEM((2, VR, KEYS), BF16),
            pltpu.VMEM((KEYS, HD), BF16),
            pltpu.VMEM((KEYS, UNIT), F32),
            pltpu.VMEM((KEYS, UNIT), F32),
            pltpu.VMEM((ROWS, SPAN, 2 * HD), BF16),
            pltpu.VMEM((ROWS, SPAN, 2 * HD), BF16),
            pltpu.VMEM((2 * G * HD, 128), BF16),
            pltpu.VMEM((2, QV, HD), F32),
            pltpu.VMEM((2, NY, 2, NZ, QV, HD), BF16),
            pltpu.VMEM((8, 2, VR, HALF), BF16),
            pltpu.VMEM((8, VR, HALF), BF16),
            pltpu.VMEM((8, VR, HALF), BF16),
            pltpu.VMEM((8, VR, HALF), BF16),
            pltpu.VMEM((2, NZ, QV, 2 * HD), BF16),
            pltpu.VMEM((2, NZ, QV, 2 * HD), BF16),
            pltpu.VMEM((2, NZ, NY, 2, QV, HD), BF16),
            pltpu.VMEM((NZ * NY * 2 * QV, HD), F32),
            pltpu.VMEM((2, QV, HD), F32),
            pltpu.VMEM((2, QV, HD), F32),
            pltpu.VMEM((384, 128), F32),
            pltpu.VMEM((4, 96, 128), F32),
            sem((7,)),
            sem((2, 8)), sem((2, 8)), sem((8,)), sem((8,)), sem((8,)), sem((8,)),
            sem((8,)), sem((8,)), sem((8,)), sem((8,)), sem((2, 8)), sem((2, 8)),
            sem((2, 8)), sem((2, 8)), sem((2, 4)), sem((2, 4)), sem((2, 4)), sem((2, 4)),
            sem((4,)), sem((4,)),
        ],
        compiler_params=pltpu.CompilerParams(
            collective_id=0, has_side_effects=True, vmem_limit_bytes=60 * 2**20
        ),
    )(queries, keys, values, kept.reshape(-1, 128), suffix_keys, suffix_values, lengths, out_weight)


def solution(mesh):
    return jax.shard_map(
        per_device,
        mesh=mesh,
        in_specs=(
            P("kv", "tp"),
            P("kv", "tp"),
            P("kv", "tp"),
            P("kv"),
            P("kv", None, "tp"),
            P("kv", None, "tp"),
            P("kv"),
            P("tp", "kv"),
        ),
        out_specs=P("tp", "kv"),
        check_vma=False,
    )
```

time: 554 us -> 86.5 us (0.16)
  waiting for transfers between devices: 267 us -> 0 us
  matrix products: 115 us -> 0 us
  Pallas kernels: 0 us -> 84.9 us
  other arithmetic: 73.8 us -> 0 us
  local copies, waits for them, and re-layouts: 64.2 us -> 1.35 us
  starting transfers between devices: 16.9 us -> 0 us
  between operations: 13.2 us -> 0.01 us
    all_gather x2 -> x0, waiting for transfers between devices: 143 us -> none  [the longest x1 75.4 us: per_device(): attention = lax.all_gather(merged, 'kv', axis=0, tiled=True)]
    dot_general x27 -> x0, matrix products: 115 us -> none  [the longest x12 73.2 us: one_block(): jnp.einsum('rhgd,khd->rhgk', query_grouped, keys3, preferred_element_type...]
    all_to_all x3 -> x0, waiting for transfers between devices: 105 us -> none  [the longest x1 84.5 us: per_device(): lax.all_to_all(numer_p, 'kv', split_axis=0, concat_axis=0, tiled=True)]
    pallas_call x0 -> x1, Pallas kernels: none -> 84.9 us  [per_device(): pl.pallas_call(kernel, out_shape=jax.ShapeDtypeStruct((96, 128), BF16), i...]
    reduce_sum x15 -> x0, other arithmetic: 70.2 us -> none  [the longest x12 64.5 us: one_block(): denom = jnp.sum(weights.astype(jnp.float32), axis=-1)]
    while x52 -> x0, local copies, waits for them, and re-layouts: 25.2 us -> none
    reduce_scatter x1 -> x0, waiting for transfers between devices: 18.2 us -> none  [per_device(): lax.psum_scatter(jnp.dot(attention, out_weight, preferred_element_type=jn...]
    all_to_all x3 -> x0, starting transfers between devices: 16.6 us -> none  [the longest x1 6.62 us: per_device(): lax.all_to_all(denom_p, 'kv', split_axis=0, concat_axis=0, tiled=True)]
  transfers between devices with their start and end apart: 6 -> 0, of which waited for: 6 -> 0; matrix products, arithmetic and copies ran while one was open for 5% -> 0% of each run, Pallas kernels for 0% -> 0%
where the time goes in v1:
time: 86.5 us; the launch traced here: 86.3 us
  Pallas kernels  84.9 us (98%)
  local copies, waits for them, and re-layouts  1.35 us (2%)
    pallas_call x1, Pallas kernels, per_device(): pl.pallas_call(kernel, out_shape=jax.ShapeDtypeStruct((96, 128), BF16), i...  84.9 us

profile of v1, /device:TPU:1, one launch (start us, length us, event | category | flops | bytes accessed | tf_op | source)
XLA Modules:
  0.0 86.3 jit_solution(9888357321250807521)
XLA Ops:
  0.0 84.9 %shard_map.82 = bf16[96,128]{1,0:T(8,128)(2,1)} custom-call(bf16[6,2048]{1,0:T(8,128)(2,1)} %q_ref.1, bf16[4096,256]{1,0:T(8,128)(2,1)} %k_hbm.1, bf16[4096,256]{1,0:T(8,128)(2,1)} %v_hbm.1, s32[32,128]{1,0:T(8,128)} %bitcast.1, bf16[6,512,256]{2,1,0:T(8,128)(2,1)} %sk_hbm.1, bf16[6,512,256]{2,1,0:T(8,128)(2,1)} %sv_hbm.1, s32[6]{0:T(128)} %len_ref.1, ...), custom_call_target="tpu_custom_call" | custom-call | tf_op jit(solution)/shard_map/pallas_call | solution.py:405
  84.9 1.3 %copy.10 = bf16[96,128]{1,0:T(8,128)(2,1)} copy(bf16[96,128]{1,0:T(8,128)(2,1)} %shard_map.82) | data formatting | bytes 49152

commit v2 on v1

--- a/solution.py
+++ b/solution.py
@@ -55,15 +55,10 @@
     return x[:HD], x[HD : HD + 1] + x[HD + 1 : HD + 2] + x[HD + 2 : HD + 3]
 
 
-def unpack_r(x):
-    x = x.astype(F32)
-    return x[:, :HD], x[:, HD : HD + 1] + x[:, HD + 1 : HD + 2] + x[:, HD + 2 : HD + 3]
-
-
 def kernel(
     q_ref, k_hbm, v_hbm, kept_ref, sk_hbm, sv_hbm, len_ref, w_hbm, out_ref,
     kbuf, vbuf, vt, bias, s0, s1, skbuf, svbuf, wbuf, qf, qg, rsout, sibin, ysend, yin, zout, zin,
-    attg, attf, osuf, lsuf, part, tpin,
+    attg, attf, osuf, lsuf, part, half, tpin,
     load_sem, qz_s, qz_r, qy_s, qy_r, qs_s, qs_r, sib_s, sib_r, ry_s, ry_r, rz_s, rz_r,
     az_s, az_r, ay_s, ay_r, as_s, as_r, tp_s, tp_r,
 ):
@@ -81,6 +76,14 @@
             src_ref=src, dst_ref=dst, send_sem=s, recv_sem=r, device_id=to, device_id_type=MESH
         )
 
+    barrier = pltpu.get_barrier_semaphore()
+    peers = [sibling]
+    peers += [dev((z + i) % NZ, y, c) for i in (4, 3, 5, 2, 6, 1, 7)]
+    peers += [dev(z, (y + i) % NY, c) for i in (2, 1, 3)]
+    peers += [(k, (x + i) % 4) for i in range(1, 4)]
+    for p in peers:
+        pl.semaphore_signal(barrier, inc=1, device_id=p, device_id_type=MESH)
+
     loads = [
         pltpu.make_async_copy(sk_hbm, skbuf, load_sem.at[0]),
         pltpu.make_async_copy(sv_hbm, svbuf, load_sem.at[1]),
@@ -90,8 +93,8 @@
         loads.append(pltpu.make_async_copy(v_hbm.at[:, cols], vbuf.at[h], load_sem.at[2 + 2 * h]))
         loads.append(pltpu.make_async_copy(k_hbm.at[:, cols], kbuf.at[h], load_sem.at[3 + 2 * h]))
     loads.append(pltpu.make_async_copy(w_hbm, wbuf, load_sem.at[6]))
-    for copy in loads:
-        copy.start()
+    for i in (2, 4, 0, 1, 3, 5, 6):
+        loads[i].start()
 
     own = q_ref[...].astype(F32)
     for h in range(2):
@@ -100,51 +103,6 @@
             qf[h, pl.ds(g, ROWS, stride=G), :] = own[:, at : at + HD]
         qg[h, y, c, z] = qf[h].astype(BF16)
 
-    barrier = pltpu.get_barrier_semaphore()
-    peers = [sibling]
-    peers += [dev(z, (y + i) % NY, c) for i in range(1, NY)]
-    peers += [dev((z + i) % NZ, y, c) for i in range(1, NZ)]
-    peers += [(k, (x + i) % 4) for i in range(1, 4)]
-    for p in peers:
-        pl.semaphore_signal(barrier, inc=1, device_id=p, device_id_type=MESH)
-    pl.semaphore_wait(barrier, len(peers))
-
-    def qz(h, i):
-        blk = qg.at[h, y, c, z]
-        return remote(blk, blk, qz_s.at[h, i], qz_r.at[h, i], dev((z + i) % NZ, y, c))
-
-    def qz_arrival(h, i):
-        blk = qg.at[h, y, c, (z + NZ - i) % NZ]
-        return remote(blk, blk, qz_s.at[h, i], qz_r.at[h, i], dev((z + i) % NZ, y, c))
-
-    def unit_offset(s):
-        j = (s + s // 4) % 4
-        return j + (j // 2) * (5 - 2 * j)
-
-    def qy(s):
-        blk = qg.at[s // 4, y, c]
-        return remote(blk, blk, qy_s.at[s], qy_r.at[s], dev(z, (y + NY - unit_offset(s)) % NY, c))
-
-    def qy_arrival(s):
-        blk = qg.at[s // 4, (y + unit_offset(s)) % NY, c]
-        return remote(blk, blk, qy_s.at[s], qy_r.at[s], sibling)
-
-    def qs(s):
-        blk = qg.at[s // 4, (y + unit_offset(s)) % NY, c]
-        return remote(blk, blk, qs_s.at[s], qs_r.at[s], sibling)
-
-    def qs_arrival(s):
-        blk = qg.at[s // 4, (y + unit_offset(s)) % NY, 1 - c]
-        return remote(blk, blk, qs_s.at[s], qs_r.at[s], sibling)
-
-    def forward(s):
-        qy_arrival(s).wait_recv()
-        qs(s).start()
-
-    for h in range(2):
-        for i in (1, 7, 2, 6, 3, 5, 4):
-            qz(h, i).start()
-
     kept = jnp.where(kept_ref[...] > 0, 0.0, DROPPED).astype(F32)
     kept = jnp.concatenate([kept, jnp.zeros((HD - KEYS // HD, HD), F32)], axis=0).T
     for j in range(KEYS // HD):
@@ -161,18 +119,62 @@
         lax.fori_loop(0, KEYS // 512, turn, 0)
         vt[h, HD:, :] = jnp.ones((VR - HD, KEYS), BF16)
 
+    pl.semaphore_wait(barrier, len(peers))
+
+    def qz(h, i):
+        blk = qg.at[h, y, c, z]
+        return remote(blk, blk, qz_s.at[h, i], qz_r.at[h, i], dev((z + i) % NZ, y, c))
+
+    def qz_arrival(h, i):
+        blk = qg.at[h, y, c, (z + NZ - i) % NZ]
+        return remote(blk, blk, qz_s.at[h, i], qz_r.at[h, i], dev((z + i) % NZ, y, c))
+
+    def unit_offset(s):
+        return (s + s // 4) % NY
+
+    def qy(s, zz):
+        blk = qg.at[s // 4, y, c, zz]
+        return remote(blk, blk, qy_s.at[s], qy_r.at[s], dev(z, (y + NY - unit_offset(s)) % NY, c))
+
+    def qy_all(s):
+        blk = qg.at[s // 4, (y + unit_offset(s)) % NY, c]
+        return remote(blk, blk, qy_s.at[s], qy_r.at[s], sibling)
+
+    def qs_own(s, zz):
+        blk = qg.at[s // 4, y, c, zz]
+        return remote(blk, blk, qs_s.at[s], qs_r.at[s], sibling)
+
+    def qs(s):
+        blk = qg.at[s // 4, (y + unit_offset(s)) % NY, c]
+        return remote(blk, blk, qs_s.at[s], qs_r.at[s], sibling)
+
+    def qs_arrival(s):
+        blk = qg.at[s // 4, (y + unit_offset(s)) % NY, 1 - c]
+        return remote(blk, blk, qs_s.at[s], qs_r.at[s], sibling)
+
+    def forward(s):
+        qy_all(s).wait_recv()
+        qs(s).start()
+
+    def relay(h, i):
+        if i:
+            qz_arrival(h, i).wait_recv()
+        zz = (z + NZ - i) % NZ
+        qs_own(7 * h, zz).start()
+        for s in (1, 3, 2):
+            qy(3 * h + s, zz).start()
+
     def spread(h):
-        for i in range(1, NZ):
-            qz_arrival(h, i).wait_recv()
-        qs(7 * h).start()
-        for s in (1, 2, 3):
-            qy(3 * h + s).start()
+        for i in (4, 3, 5, 2, 6, 1, 7):
+            qz(h, i).start()
+        relay(h, 0)
 
     spread(0)
 
     loads[0].wait()
     loads[1].wait()
-    for r in range(ROWS):
+
+    def suffix(r):
         live = lax.broadcasted_iota(jnp.int32, (G, SPAN), 1) < len_ref[r]
         for h in range(2):
             cols = slice(h * HD, (h + 1) * HD)
@@ -186,10 +188,19 @@
             osuf[h, r * G : (r + 1) * G, :] = o * (1.0 / total)
             lsuf[h, r * G : (r + 1) * G, :] = jnp.broadcast_to(top + jnp.log2(total), (G, HD))
 
+    suffix(0)
+    suffix(1)
+    relay(0, 1)
+    relay(0, 7)
+    suffix(2)
+    suffix(3)
+    for i in (2, 6, 3, 5, 4):
+        relay(0, i)
     spread(1)
+    suffix(4)
+    suffix(5)
     loads[3].wait()
     loads[5].wait()
-    forward(1)
     qs_arrival(0).wait_recv()
 
     first_lane = (lax.broadcasted_iota(jnp.int32, (UNIT, HD), 1) == 0).astype(F32).astype(BF16)
@@ -209,13 +220,12 @@
         return jnp.full((8, UNIT), -3e38, F32)
 
     def stage(s, buf, nxt, m8):
-        last = isinstance(s, int) and s == 7
         top = jnp.max(m8, axis=0, keepdims=True) * C
-        q = None if last else unit_queries(s + 1)
+        q = None if nxt is None else unit_queries(s + 1)
         o = jnp.zeros((VR, UNIT), F32)
         m_next = lowest()
         for t in range(KEYS // TK):
-            if not last:
+            if nxt is not None:
                 m_next = scores(s + 1, q, t, nxt, m_next)
             rows = slice(t * TK, (t + 1) * TK)
             p = jnp.exp2(buf[rows, :] * C - top).astype(BF16)
@@ -247,10 +257,12 @@
             y_send(3 * h + s).wait_recv()
             parts.append(unpack_t(yin[3 * h + s]))
         o, lse = merge(parts)
-        hi, mid, lo = split3(jnp.broadcast_to(lse, (HD, HALF)).T)
-        lane = lax.broadcasted_iota(jnp.int32, (HALF, HD), 1)
-        stat = jnp.where(lane == 0, hi, jnp.where(lane == 1, mid, jnp.where(lane == 2, lo, 0.0)))
-        zout[h] = jnp.concatenate([o.T, stat], axis=1).astype(BF16).reshape(NZ, QV, 2 * HD)
+        stat = jnp.concatenate(list(split3(lse)) + [jnp.zeros((13, HALF), F32)], axis=0)
+        rows = o.T.astype(BF16)
+        for zz in range(NZ):
+            zout[h, zz, :QV, :] = rows[zz * QV : (zz + 1) * QV]
+            turned = stat if zz == 0 else pltpu.roll(stat, HALF - zz * QV, axis=1)
+            zout[h, zz, QV:, :] = turned[:, :HD].astype(BF16)
         for i in (4, 3, 5, 2, 6, 1, 7):
             z_send(h, i).start()
 
@@ -263,21 +275,29 @@
         return remote(blk, blk, az_s.at[h, i], az_r.at[h, i], dev((z + i) % NZ, y, c))
 
     def z_merge(h):
-        parts = [(osuf[h], lsuf[h][:, :1]), unpack_r(zout[h, z])]
         for i in range(1, NZ):
             z_send(h, i).wait_recv()
-            parts.append(unpack_r(zin[h, i]))
+        got = [zout[h, z]] + [zin[h, i] for i in range(1, NZ)]
+        stats = [g[QV:].astype(F32) for g in got]
+        lse = jnp.concatenate([st[0:1] + st[1:2] + st[2:3] for st in stats], axis=0).T
+        parts = [(g[:QV].astype(F32), lse[:QV, i : i + 1]) for i, g in enumerate(got)]
+        parts.append((osuf[h], lsuf[h][:, :1]))
         attg[h, z, y, c] = merge(parts)[0].astype(BF16)
         for i in (4, 3, 5, 2, 6, 1, 7):
             az(h, i).start()
-
-    def ay(h, i):
-        blk = attg.at[h, :, y, c]
+        a_relay(h, 0)
+
+    def ay(h, i, zz):
+        blk = attg.at[h, zz, y, c]
         return remote(blk, blk, ay_s.at[h, i], ay_r.at[h, i], dev(z, (y + NY - i) % NY, c))
 
-    def ay_arrival(h, i):
+    def ay_all(h, i):
         blk = attg.at[h, :, (y + i) % NY, c]
         return remote(blk, blk, ay_s.at[h, i], ay_r.at[h, i], sibling)
+
+    def a_own(h, zz):
+        blk = attg.at[h, zz, y, c]
+        return remote(blk, blk, as_s.at[h, 0], as_r.at[h, 0], sibling)
 
     def a_sib(h, i):
         blk = attg.at[h, :, (y + i) % NY, c]
@@ -287,16 +307,21 @@
         blk = attg.at[h, :, (y + i) % NY, 1 - c]
         return remote(blk, blk, as_s.at[h, i], as_r.at[h, i], sibling)
 
+    def a_relay(h, i):
+        if i:
+            az_arrival(h, i).wait_recv()
+        zz = (z + NZ - i) % NZ
+        for j in (2, 1, 3):
+            ay(h, j, zz).start()
+        a_own(h, zz).start()
+
     def gather_y(h):
-        for i in range(1, NZ):
-            az_arrival(h, i).wait_recv()
-        for i in (2, 1, 3):
-            ay(h, i).start()
-        a_sib(h, 0).start()
+        for i in (1, 7, 2, 6, 3, 5, 4):
+            a_relay(h, i)
 
     def gather_core(h):
         for i in (1, 3, 2):
-            ay_arrival(h, i).wait_recv()
+            ay_all(h, i).wait_recv()
             a_sib(h, i).start()
 
     def project(h):
@@ -307,93 +332,93 @@
         att = jnp.concatenate([attf[pl.ds(g, rows, stride=G), :].astype(BF16) for g in range(G)], axis=1)
         return jnp.dot(att, wbuf[h * G * HD : (h + 1) * G * HD, :], preferred_element_type=F32)
 
-    q = unit_queries(0)
-    m8 = lowest()
-    for t in range(KEYS // TK):
-        m8 = scores(0, q, t, s0, m8)
+    def all_scores(s, buf):
+        q = unit_queries(s)
+        m8 = lowest()
+        for t in range(KEYS // TK):
+            m8 = scores(s, q, t, buf, m8)
+        return m8
+
+    m8 = all_scores(0, s0)
+    forward(1)
+    stage(0, s0, None, m8)
+    for i in (1, 7, 2, 6, 3, 5, 4):
+        relay(1, i)
+    forward(2)
+    qs_arrival(1).wait_recv()
+    m8 = all_scores(1, s0)
 
     def pair(it, m8):
-        a = 2 * it
+        a = 2 * it + 1
         b = a + 1
-        pl.when(it <= 2)(lambda: forward(a + 2))
         qs_arrival(b).wait_recv()
+        pl.when(it <= 1)(lambda: forward(b + 1))
         m8 = stage(a, s0, s1, m8)
-
-        @pl.when(it >= 1)
-        def _():
-            sib_merge(a - 1)
-            y_send(a - 1).start()
-
-        @pl.when(it == 3)
-        def _():
-            z_merge(0)
-
-        @pl.when(it <= 1)
-        def _():
-            forward(b + 2)
-
-        @pl.when(it <= 2)
-        def _():
-            qs_arrival(a + 2).wait_recv()
-
+        sib_merge(a - 1)
+        pl.when(it >= 1)(lambda: y_send(a - 1).start())
+        qs_arrival(b + 1).wait_recv()
+        pl.when(it <= 1)(lambda: forward(b + 2))
+        if isinstance(it, int):
+            y_merge(0)
         m8 = stage(b, s1, s0, m8)
         sib_merge(a)
-
-        @pl.when(it >= 1)
-        def _():
-            y_send(a).start()
-
-        @pl.when(it == 2)
-        def _():
-            y_merge(0)
-
+        y_send(a).start()
         return m8
 
-    pair(3, lax.fori_loop(0, 3, pair, m8))
-
-    gather_y(0)
+    m8 = pair(2, lax.fori_loop(0, 2, pair, m8))
+    sib_merge(6)
+    y_send(6).start()
+    stage(7, s0, None, m8)
+    z_merge(0)
     sib_merge(7)
     y_merge(1)
-    gather_core(0)
-    loads[6].wait()
-    part[...] = project(0)
-    z_merge(1)
-    gather_y(1)
-    gather_core(1)
-    part[...] += project(1)
-
-    per = part.shape[0] // 4
-
-    def mine(xx):
-        return part.at[pl.ds(pl.multiple_of(xx * per, 8), per), :]
-
-    def tp_send(i):
-        to = (x + i) % 4
-        return remote(mine(to), tpin.at[i], tp_s.at[i], tp_r.at[i], (k, to))
-
-    for i in range(1, 4):
-        tp_send(i).start()
-    total = part[pl.ds(pl.multiple_of(x * per, 8), per), :]
-    for i in range(1, 4):
-        tp_send(i).wait_recv()
-        total = total + tpin[i]
-    out_ref[...] = total.astype(BF16)
-
+    gather_y(0)
     for h in range(2):
         for i in range(1, NZ):
             qz(h, i).wait_send()
-            z_send(h, i).wait_send()
-            az(h, i).wait_send()
-        for i in range(1, NY):
-            ay(h, i).wait_send()
-        for i in range(NY):
-            a_sib(h, i).wait_send()
+            if h == 0:
+                z_send(0, i).wait_send()
     for s in range(8):
         qs(s).wait_send()
         sib_send(s).wait_send()
         if 1 <= s <= 6:
-            qy(s).wait_send()
+            qy_all(s).wait_send()
             y_send(s).wait_send()
+    loads[6].wait()
+    z_merge(1)
+    gather_core(0)
+    part[...] = project(0)
+    gather_y(1)
+    for h in range(2):
+        for i in range(1, NZ):
+            az(h, i).wait_send()
+            if h == 1:
+                z_send(1, i).wait_send()
+    gather_core(1)
+    part[...] += project(1)
+    half[...] = part[...].astype(BF16)
+
+    per = part.shape[0] // 4
+
+    def mine(xx):
+        return half.at[pl.ds(pl.multiple_of(xx * per, 32), per), :]
+
+    def tp_send(i):
+        to = (x + i) % 4
+        return remote(mine(to), tpin.at[i], tp_s.at[i], tp_r.at[i], (k, to))
+
+    for i in range(1, 4):
+        tp_send(i).start()
+    for h in range(2):
+        for i in range(1, NY):
+            ay_all(h, i).wait_send()
+        for i in range(NY):
+            a_sib(h, i).wait_send()
+    total = part[pl.ds(pl.multiple_of(x * per, 8), per), :]
+    for i in range(1, 4):
+        tp_send(i).wait_recv()
+        total = total + tpin[i].astype(F32)
+    out_ref[...] = total.astype(BF16)
     for i in range(1, 4):
         tp_send(i).wait_send()
 
@@ -426,14 +451,15 @@
             pltpu.VMEM((8, VR, HALF), BF16),
             pltpu.VMEM((8, VR, HALF), BF16),
             pltpu.VMEM((8, VR, HALF), BF16),
-            pltpu.VMEM((2, NZ, QV, 2 * HD), BF16),
-            pltpu.VMEM((2, NZ, QV, 2 * HD), BF16),
+            pltpu.VMEM((2, NZ, QV + 16, HD), BF16),
+            pltpu.VMEM((2, NZ, QV + 16, HD), BF16),
             pltpu.VMEM((2, NZ, NY, 2, QV, HD), BF16),
             pltpu.VMEM((NZ * NY * 2 * QV, HD), F32),
             pltpu.VMEM((2, QV, HD), F32),
             pltpu.VMEM((2, QV, HD), F32),
             pltpu.VMEM((384, 128), F32),
-            pltpu.VMEM((4, 96, 128), F32),
+            pltpu.VMEM((384, 128), BF16),
+            pltpu.VMEM((4, 96, 128), BF16),
             sem((7,)),
             sem((2, 8)), sem((2, 8)), sem((8,)), sem((8,)), sem((8,)), sem((8,)),
             sem((8,)), sem((8,)), sem((8,)), sem((8,)), sem((2, 8)), sem((2, 8)),

time: 86.5 us -> 78.3 us (0.905)
  Pallas kernels: 84.9 us -> 76.7 us
    pallas_call x1, Pallas kernels: 84.9 us -> 76.7 us  [per_device(): pl.pallas_call(kernel, out_shape=jax.ShapeDtypeStruct((96, 128), BF16), i...]
where the time goes in v2:
time: 78.3 us; the launch traced here: 78.1 us
  Pallas kernels  76.7 us (98%)
  local copies, waits for them, and re-layouts  1.35 us (2%)
    pallas_call x1, Pallas kernels, per_device(): pl.pallas_call(kernel, out_shape=jax.ShapeDtypeStruct((96, 128), BF16), i...  76.7 us

profile of v2, /device:TPU:1, one launch (start us, length us, event | category | flops | bytes accessed | tf_op | source)
XLA Modules:
  0.0 78.1 jit_solution(6845647789229739298)
XLA Ops:
  0.0 76.7 %shard_map.82 = bf16[96,128]{1,0:T(8,128)(2,1)} custom-call(bf16[6,2048]{1,0:T(8,128)(2,1)} %q_ref.1, bf16[4096,256]{1,0:T(8,128)(2,1)} %k_hbm.1, bf16[4096,256]{1,0:T(8,128)(2,1)} %v_hbm.1, s32[32,128]{1,0:T(8,128)} %bitcast.1, bf16[6,512,256]{2,1,0:T(8,128)(2,1)} %sk_hbm.1, bf16[6,512,256]{2,1,0:T(8,128)(2,1)} %sv_hbm.1, s32[6]{0:T(128)} %len_ref.1, ...), custom_call_target="tpu_custom_call" | custom-call | tf_op jit(solution)/shard_map/pallas_call | solution.py:430
  76.7 1.3 %copy.10 = bf16[96,128]{1,0:T(8,128)(2,1)} copy(bf16[96,128]{1,0:T(8,128)(2,1)} %shard_map.82) | data formatting | bytes 49152

commit v3 on v2

--- a/solution.py
+++ b/solution.py
@@ -161,8 +161,13 @@
             qz_arrival(h, i).wait_recv()
         zz = (z + NZ - i) % NZ
         qs_own(7 * h, zz).start()
-        for s in (1, 3, 2):
+        for s in (1, 3):
             qy(3 * h + s, zz).start()
+
+    def qy_far(h):
+        blk = qg.at[h, y, c]
+        s = 3 * h + 2
+        return remote(blk, blk, qy_s.at[s], qy_r.at[s], dev(z, (y + 2) % NY, c))
 
     def spread(h):
         for i in (4, 3, 5, 2, 6, 1, 7):
@@ -196,6 +201,7 @@
     suffix(3)
     for i in (2, 6, 3, 5, 4):
         relay(0, i)
+    qy_far(0).start()
     spread(1)
     suffix(4)
     suffix(5)
@@ -344,6 +350,7 @@
     stage(0, s0, None, m8)
     for i in (1, 7, 2, 6, 3, 5, 4):
         relay(1, i)
+    qy_far(1).start()
     forward(2)
     qs_arrival(1).wait_recv()
     m8 = all_scores(1, s0)
@@ -352,20 +359,28 @@
         a = 2 * it + 1
         b = a + 1
         qs_arrival(b).wait_recv()
-        pl.when(it <= 1)(lambda: forward(b + 1))
+        forward(b + 1)
         m8 = stage(a, s0, s1, m8)
         sib_merge(a - 1)
         pl.when(it >= 1)(lambda: y_send(a - 1).start())
         qs_arrival(b + 1).wait_recv()
-        pl.when(it <= 1)(lambda: forward(b + 2))
-        if isinstance(it, int):
-            y_merge(0)
+        forward(b + 2)
         m8 = stage(b, s1, s0, m8)
         sib_merge(a)
         y_send(a).start()
         return m8
 
-    m8 = pair(2, lax.fori_loop(0, 2, pair, m8))
+    m8 = lax.fori_loop(0, 2, pair, m8)
+    qs_arrival(6).wait_recv()
+    m8 = stage(5, s0, s1, m8)
+    sib_merge(4)
+    y_send(4).start()
+    y_merge(0)
+    stage(6, s1, None, m8)
+    sib_merge(5)
+    y_send(5).start()
+    qs_arrival(7).wait_recv()
+    m8 = all_scores(7, s0)
     sib_merge(6)
     y_send(6).start()
     stage(7, s0, None, m8)
@@ -387,8 +402,8 @@
     loads[6].wait()
     z_merge(1)
     gather_core(0)
+    gather_y(1)
     part[...] = project(0)
-    gather_y(1)
     for h in range(2):
         for i in range(1, NZ):
             az(h, i).wait_send()
@@ -407,7 +422,7 @@
         to = (x + i) % 4
         return remote(mine(to), tpin.at[i], tp_s.at[i], tp_r.at[i], (k, to))
 
-    for i in range(1, 4):
+    for i in (2, 1, 3):
         tp_send(i).start()
     for h in range(2):
         for i in range(1, NY):

time: 78.3 us -> 76.3 us (0.974)
  Pallas kernels: 76.7 us -> 74.8 us
    pallas_call x1, Pallas kernels: 76.7 us -> 74.8 us  [per_device(): pl.pallas_call(kernel, out_shape=jax.ShapeDtypeStruct((96, 128), BF16), i...]
where the time goes in v3:
time: 76.3 us; the launch traced here: 76.1 us
  Pallas kernels  74.8 us (98%)
  local copies, waits for them, and re-layouts  1.35 us (2%)
    pallas_call x1, Pallas kernels, per_device(): pl.pallas_call(kernel, out_shape=jax.ShapeDtypeStruct((96, 128), BF16), i...  74.8 us

profile of v3, /device:TPU:1, one launch (start us, length us, event | category | flops | bytes accessed | tf_op | source)
XLA Modules:
  0.0 76.1 jit_solution(9953345707611974530)
XLA Ops:
  0.0 74.8 %shard_map.82 = bf16[96,128]{1,0:T(8,128)(2,1)} custom-call(bf16[6,2048]{1,0:T(8,128)(2,1)} %q_ref.1, bf16[4096,256]{1,0:T(8,128)(2,1)} %k_hbm.1, bf16[4096,256]{1,0:T(8,128)(2,1)} %v_hbm.1, s32[32,128]{1,0:T(8,128)} %bitcast.1, bf16[6,512,256]{2,1,0:T(8,128)(2,1)} %sk_hbm.1, bf16[6,512,256]{2,1,0:T(8,128)(2,1)} %sv_hbm.1, s32[6]{0:T(128)} %len_ref.1, ...), custom_call_target="tpu_custom_call" | custom-call | tf_op jit(solution)/shard_map/pallas_call | solution.py:445
  74.8 1.3 %copy.10 = bf16[96,128]{1,0:T(8,128)(2,1)} copy(bf16[96,128]{1,0:T(8,128)(2,1)} %shard_map.82) | data formatting | bytes 49152
